TPU v7x, 32 devices: a whole 2x2x4 slice. The times are simulated.
32 devices in a mesh: orb: 4 (over y, core), grp: 8 (over z, x).
Axes of the slice: x: 2, y: 2, z: 4, core: 2. Of those that a mesh axis runs over, the one named last changes fastest.
Arguments:
- targets: bfloat16 [4, 98304], P('orb'), may hold values from -6 to 6
- partners: bfloat16 [64, 98304], P(('orb', 'grp')), may hold values from -6 to 6
Outputs:
- exchange: float32 [4, 98304], P('orb', 'grp')
All inputs are finite; a program needn't handle non-finite values.
Results may differ from a plain program's by a relative error of at most 0.007.
Values may be sent and summed in bfloat16 or wider, within the bound.
A program may use at most 64 MiB of HBM per device.

v0:
```python
import math

import jax
import jax.numpy as jnp
from jax import lax
from jax.sharding import PartitionSpec as P

X = 32
Y = 48
Z = 64
STEPS = 3


screening = 0.11
spacing = 0.45


def from_behind(block, axis, distance):
    devices = range(lax.axis_size(axis))
    route = [((i - distance) % len(devices), i) for i in devices]
    return lax.ppermute(block, axis, route)


def hartley(length):
    indices = jnp.arange(length, dtype=jnp.int32)
    product = indices[:, None] * indices[None, :] % length
    angles = 2.0 * math.pi / length * product.astype(jnp.float32)
    return (jnp.cos(angles) + jnp.sin(angles)).astype(jnp.bfloat16)


def block_hartley(length, copies):
    indices = jnp.arange(length * copies, dtype=jnp.int32)
    same_block = indices[:, None] // length == indices[None, :] // length
    product = indices[:, None] % length * (indices[None, :] % length) % length
    angles = 2.0 * math.pi / length * product.astype(jnp.float32)
    values = jnp.cos(angles) + jnp.sin(angles)
    return jnp.where(same_block, values, 0.0).astype(jnp.bfloat16)


def squared_wave(length):
    indices = jnp.arange(length, dtype=jnp.int32)
    folded = jnp.minimum(indices, length - indices).astype(jnp.float32)
    wavenumber = 2.0 * math.pi / (length * spacing) * folded
    return wavenumber * wavenumber


def coulomb_table():
    squares = (
        squared_wave(X)[:, None, None]
        + squared_wave(Y)[None, :, None]
        + squared_wave(Z)[None, None, :]
    )
    positive = squares > 0.0
    guarded = jnp.where(positive, squares, 1.0)
    screened = 4.0 * math.pi * (1.0 - jnp.exp(-guarded / (4.0 * screening * screening))) / guarded
    kernel = jnp.where(positive, screened, math.pi / (screening * screening))
    spread = jnp.sqrt(jnp.mean(kernel * kernel))
    return kernel / (spread * (X * Y * Z))


def contract(table, field, axis_number):
    return lax.dot_general(
        table, field, (((1,), (axis_number,)), ((), ())), preferred_element_type=jnp.float32
    ).astype(jnp.bfloat16)


def exchange_terms(target_rows, partner_rows, tables):
    table_x, table_y, block_z, kernel_table = tables
    trials = target_rows.shape[0]
    copies = partner_rows.shape[0]
    partner_grid = jnp.transpose(partner_rows.reshape(copies, X, Y, Z), (1, 2, 0, 3)).astype(
        jnp.float32
    )
    target_grid = target_rows.reshape(trials, X, Y, 1, Z).astype(jnp.float32)
    density = (
        (target_grid * partner_grid[None]).astype(jnp.bfloat16).reshape(trials, X, Y, copies * Z)
    )
    density = jnp.dot(density, block_z, preferred_element_type=jnp.float32).astype(jnp.bfloat16)
    density = contract(table_x, density, 1)
    density = contract(table_y, density, 2)
    scaled = (density.astype(jnp.float32) * kernel_table).astype(jnp.bfloat16)
    scaled = jnp.dot(scaled, block_z, preferred_element_type=jnp.float32).astype(jnp.bfloat16)
    scaled = contract(table_y, scaled, 0)
    scaled = contract(table_x, scaled, 1)
    potential = scaled.reshape(X, Y, trials, copies, Z).astype(jnp.float32)
    return jnp.sum(potential * partner_grid[:, :, None], axis=3)


def partner_sets(partners):
    received = [partners]
    for step_index in range(1, STEPS):
        received.append(from_behind(received[-1], "orb", 1))
    return received


def slab_rows(summed, trials):
    planes = summed.shape[0]
    return jnp.transpose(summed.reshape(planes, Y, trials, Z), (2, 0, 1, 3)).reshape(
        trials, planes * Y * Z
    )


def local(targets, partners):
    copies = partners.shape[0]
    trials = targets.shape[0]
    kernel_table = jnp.tile(jnp.transpose(coulomb_table(), (1, 0, 2)), (1, 1, copies))[
        :, :, None, :
    ]
    tables = (hartley(X), hartley(Y), block_hartley(Z, copies), kernel_table)
    received = partner_sets(partners)
    factor = -1.0 / math.sqrt(STEPS * lax.axis_size("grp") * copies)
    running = exchange_terms(targets, received[0], tables)
    for step_index in range(1, STEPS):
        running = running + exchange_terms(targets, received[step_index], tables)
    summed = lax.psum_scatter(
        running.reshape(X, Y * trials * Z), "grp", scatter_dimension=0, tiled=True
    )
    result = factor * slab_rows(summed, trials)
    return result


def solution(mesh):
    in_specs = (P("orb", None), P(("orb", "grp"), None))
    out_specs = P("orb", "grp")
    return jax.shard_map(local, mesh=mesh, in_specs=in_specs, out_specs=out_specs, check_vma=False)
```

profile of v0, /device:TPU:0, one launch (start us, length us, event | category | flops | bytes accessed | tf_op | source)
XLA Modules:
  0.0 157.5 jit_solution(12905950678078198888)
XLA Ops:
  6.5 0.5 collective-permute-start
  7.1 1.0 fusion.30
  8.1 1.4 reshape.365
  10.3 1.1 convert_reduce_fusion
  11.6 1.1 copy.34
  12.8 1.8 %collective-permute-done = bf16[2,98304]{1,0:T(2,128)(2,1)S(1)} collective-permute-done((bf16[2,98304]{1,0:T(2,128)(2,1)}, bf16[2,98304]{1,0:T(2,128)(2,1)S(1)}, u32[]{:S(2)}, u32[]{:S(2)}) %collective-permute-start) | collective-permute-done | bytes 393248 | tf_op jit(solution)/shard_map/ppermute | solution.py:21
  14.6 0.8 collective-permute-start.1
  15.4 0.4 fusion.24
  15.8 0.9 tile.8
  16.7 1.8 %tile.9 = f32[48,32,128]{2,0,1:T(8,128)} reshape(f32[48,32,2,64]{3,2,0,1:T(2,128)S(1)} %tile.8) | data formatting | bytes 1572864 | tf_op jit(solution)/shard_map/tile | solution.py:106
  18.4 0.4 reshape.366
  18.9 3.0 %collective-permute-done.1 = bf16[2,98304]{1,0:T(2,128)(2,1)} collective-permute-done((bf16[2,98304]{1,0:T(2,128)(2,1)S(1)}, bf16[2,98304]{1,0:T(2,128)(2,1)}, u32[]{:S(2)}, u32[]{:S(2)}) %collective-permute-start.1) | collective-permute-done | bytes 393248 | tf_op jit(solution)/shard_map/ppermute | solution.py:21
  21.9 2.6 %reshape.367 = f32[2,32,48,64]{3,2,1,0:T(8,128)} reshape(bf16[2,98304]{1,0:T(2,128)(2,1)} %collective-permute-done.1) | data formatting | bytes 1179648 | tf_op jit(solution)/shard_map/convert_element_type | solution.py:71
  24.5 8.5 %fusion.2 = (bf16[32,48,2,64]{3,2,0,1:T(2,128)(2,1)}, bf16[32,48,2,64]{3,2,0,1:T(2,128)(2,1)}, bf16[32,48,2,64]{3,2,0,1:T(2,128)(2,1)}) fusion(f32[2,32,48,64]{3,2,1,0:T(8,128)S(1)} %reshape.366, f32[32,48,64]{2,0,1:T(8,128)} %copy.34, f32[2,32,48,64]{3,2,1,0:T(8,128)} %reshape.367, f32[2,32,48,64]{3,2,1,0:T(8,128)S(1)} %reshape.365), kind=kLoop, calls=%fused_computation.6 | loop fusion | flops 1179648 | bytes 3932160 | tf_op jit(solution)/shard_map/convert_element_type | solution.py:76
  33.0 2.1 %reshape.359 = bf16[32,48,128]{2,0,1:T(8,128)(2,1)S(1)} reshape(bf16[32,48,2,64]{3,2,0,1:T(2,128)(2,1)} %get-tuple-element.5) | data formatting | bytes 786432 | tf_op jit(solution)/shard_map/reshape.30
  35.1 0.6 convolution_convert_fusion.11
  35.7 0.3 convolution_convert_fusion.10
  36.3 0.4 fusion.13
  36.7 0.6 convolution_convert_fusion.8
  37.3 0.4 convolution_convert_fusion.7
  37.7 1.2 fusion.10
  38.9 2.1 %reshape.360 = bf16[32,48,128]{2,0,1:T(8,128)(2,1)S(1)} reshape(bf16[32,48,2,64]{3,2,0,1:T(2,128)(2,1)} %get-tuple-element.6) | data formatting | bytes 786432 | tf_op jit(solution)/shard_map/reshape.42
  41.0 0.6 convolution_convert_fusion.5
  41.6 0.3 convolution_convert_fusion.4
  42.2 0.4 fusion.9
  42.5 0.6 convolution_convert_fusion.2
  43.1 0.4 convolution_convert_fusion.1
  43.5 1.2 fusion.6
  44.8 2.4 %reshape.358 = bf16[32,48,128]{2,0,1:T(8,128)(2,1)S(1)} reshape(bf16[32,48,2,64]{3,2,0,1:T(2,128)(2,1)} %get-tuple-element.7) | data formatting | bytes 786432 | tf_op jit(solution)/shard_map/reshape.1
  47.1 0.6 convolution_convert_fusion.17
  47.7 0.3 convolution_convert_fusion.16
  48.3 0.4 fusion.17
  48.6 0.6 convolution_convert_fusion.14
  49.2 0.4 convolution_convert_fusion.13
  49.6 1.2 fusion.14
  50.9 3.2 %reshape.362 = f32[32,48,2,64]{3,2,0,1:T(2,128)} reshape(f32[32,48,128]{2,0,1:T(8,128)} %fusion.14) | data formatting | bytes 1572864 | tf_op jit(solution)/shard_map/convert_element_type | solution.py:85
  54.0 5.3 %fusion.5 = f32[32,48,64]{2,0,1:T(8,128)} fusion(f32[32,48,2,64]{3,2,0,1:T(2,128)} %reshape.362, f32[2,32,48,64]{3,2,1,0:T(8,128)S(1)} %reshape.365), kind=kLoop, calls=%fused_computation.11 | loop fusion | flops 294912 | bytes 1966080 | tf_op jit(solution)/shard_map/reduce_sum | solution.py:86
  59.4 3.3 %reshape.364 = f32[32,48,2,64]{3,2,0,1:T(2,128)} reshape(f32[32,48,128]{2,0,1:T(8,128)} %fusion.6) | data formatting | bytes 1572864 | tf_op jit(solution)/shard_map/convert_element_type | solution.py:85
  62.6 5.3 %fusion.1 = f32[32,48,64]{2,0,1:T(8,128)} fusion(f32[32,48,2,64]{3,2,0,1:T(2,128)} %reshape.364, f32[2,32,48,64]{3,2,1,0:T(8,128)S(1)} %copy-done), kind=kLoop, calls=%fused_computation.3 | loop fusion | flops 294912 | bytes 1966080 | tf_op jit(solution)/shard_map/reduce_sum | solution.py:86
  68.0 2.5 %reshape.363 = f32[32,48,2,64]{3,2,0,1:T(2,128)S(1)} reshape(f32[32,48,128]{2,0,1:T(8,128)} %fusion.10) | data formatting | bytes 1572864 | tf_op jit(solution)/shard_map/convert_element_type | solution.py:85
  70.4 3.3 %fusion.3 = f32[32,48,64]{2,0,1:T(8,128)S(1)} fusion(f32[32,48,2,64]{3,2,0,1:T(2,128)S(1)} %reshape.363, f32[2,32,48,64]{3,2,1,0:T(8,128)S(1)} %reshape.366), kind=kLoop, calls=%fused_computation.7 | loop fusion | flops 294912 | bytes 1966080 | tf_op jit(solution)/shard_map/reduce_sum | solution.py:86
  73.8 0.2 add_add_fusion
  74.1 0.5 copy.56
  74.5 1.0 add.217
  75.6 0.6 dynamic-slice
  76.8 72.2 %all-reduce.3.cloned.1.call-done = f32[32,3072]{1,0:T(8,128)} async-done(((f32[32,3072]{1,0:T(8,128)}), f32[32,3072]{1,0:T(8,128)}) %all-reduce.3.cloned.1.call-update) | async-done | bytes 393232
  149.1 0.9 fusion.56
  150.0 0.7 copy.57
  (25 shorter events, 0.9 us)
Async XLA Ops:
  6.5 3.7 %copy-start.6 = (bf16[1,98304]{1,0:T(2,128)(2,1)S(1)}, bf16[1,98304]{1,0:T(2,128)(2,1)}, u32[]{:S(2)}) copy-start(bf16[1,98304]{1,0:T(2,128)(2,1)} %param.2) | copy-start | bytes 589828
  6.5 142.5 %all-reduce.3.cloned.1.call-start = ((), (), s32[]{:S(2)}) async-start(), calls=%async_computation | async-start | bytes 786432
  6.5 8.1 %collective-permute-start = (bf16[2,98304]{1,0:T(2,128)(2,1)}, bf16[2,98304]{1,0:T(2,128)(2,1)S(1)}, u32[]{:S(2)}, u32[]{:S(2)}) collective-permute-start(bf16[2,98304]{1,0:T(2,128)(2,1)} %param.3), channel_id=1, source_target_pairs={{24,0},{0,8},{8,16},{16,24},{25,1},{1,9},{9,17},{17,25},{26,2},{2,... | collective-permute-start | bytes 1179656 | tf_op jit(solution)/shard_map/ppermute | solution.py:21
  14.6 7.3 %collective-permute-start.1 = (bf16[2,98304]{1,0:T(2,128)(2,1)S(1)}, bf16[2,98304]{1,0:T(2,128)(2,1)}, u32[]{:S(2)}, u32[]{:S(2)}) collective-permute-start(bf16[2,98304]{1,0:T(2,128)(2,1)S(1)} %collective-permute-done), channel_id=1, source_target_pairs={{24,0},{0,8},{8,16},{16,24},{25,1},{1,9},{9,17},{17,25},{26,2},{2,... | collective-permute-start | bytes 1179656 | tf_op jit(solution)/shard_map/ppermute | solution.py:21
  35.1 1.1 copy-start.1
  41.0 1.1 copy-start.2
  47.1 1.1 copy-start.3
  59.4 3.3 %copy-start = (f32[2,32,48,64]{3,2,1,0:T(8,128)S(1)}, f32[2,32,48,64]{3,2,1,0:T(8,128)}, u32[]{:S(2)}) copy-start(f32[2,32,48,64]{3,2,1,0:T(8,128)} %reshape.367) | copy-start | bytes 2359300
  70.4 3.4 %copy-start.4 = (f32[32,48,64]{2,0,1:T(8,128)S(1)}, f32[32,48,64]{2,0,1:T(8,128)}, u32[]{:S(2)}) copy-start(f32[32,48,64]{2,0,1:T(8,128)} %fusion.5) | copy-start | bytes 1179652
  70.4 3.4 %copy-start.5 = (f32[32,48,64]{2,0,1:T(8,128)S(1)}, f32[32,48,64]{2,0,1:T(8,128)}, u32[]{:S(2)}) copy-start(f32[32,48,64]{2,0,1:T(8,128)} %fusion.1) | copy-start | bytes 1179652
  74.1 1.5 copy-start.7
Sparse Core Ops, SparseCore 0:
  75.7 73.3 all-reduce.2
where the time goes:
time: 158 us; the launch traced here: 157 us
  waiting for transfers between devices  77.1 us (49%)
  local copies, waits for them, and re-layouts  27.2 us (17%)
  other arithmetic  26.3 us (17%)
  between operations  15 us (9%)
  matrix products  10.6 us (7%)
    unnamed x2, waiting for transfers between devices  72.3 us
    reduce_sum x3, other arithmetic, exchange_terms(): return jnp.sum(potential * partner_grid[:, :, None], axis=3)  14 us
    convert_element_type x3, local copies, waits for them, and re-layouts, exchange_terms(): potential = scaled.reshape(X, Y, trials, copies, Z).astype(jnp.float32)  8.89 us
    convert_element_type x1, other arithmetic, exchange_terms(): (target_grid * partner_grid[None]).astype(jnp.bfloat16)  8.48 us
    dot_general x12, matrix products, contract(): lax.dot_general(table, field, (((1,), (axis_number,)), ((), ())), preferr...  7.01 us
    another operation x3, local copies, waits for them, and re-layouts  6.62 us
    ppermute x2, waiting for transfers between devices, from_behind(): return lax.ppermute(block, axis, route)  4.87 us
    convert_element_type x3, local copies, waits for them, and re-layouts, exchange_terms(): jnp.transpose(partner_rows.reshape(copies, X, Y, Z), (1, 2, 0, 3))  4.44 us
  transfers between devices with their start and end apart: 3, of which 3 were waited for; matrix products, arithmetic and copies ran while one was open for 6% of the time, Pallas kernels for 0%

commit v1 on v0

v1 whole, which is shorter than its diff:
```python
import functools
import math

import jax
import jax.numpy as jnp
import ml_dtypes
import numpy as np
from jax import lax
from jax.experimental import pallas as pl
from jax.experimental.pallas import tpu as pltpu
from jax.sharding import PartitionSpec as P

X = 32
Y = 48
Z = 64
STEPS = 3
LANES = 128
FOLD = LANES // Z
ROWS_Y = Y // FOLD
EIGHT = 8
GROUPS_Y = ROWS_Y // EIGHT
GROUPS = FOLD * GROUPS_Y
X_BLOCK = 4
X_BLOCKS = X // X_BLOCK
BLOCK_ROWS = X_BLOCK * EIGHT

screening = 0.11
spacing = 0.45
f32 = jnp.float32
bf16 = jnp.bfloat16


def hartley(length):
    indices = np.arange(length)
    angles = 2.0 * math.pi / length * (indices[:, None] * indices[None, :] % length)
    values = (np.cos(angles) + np.sin(angles)).astype(np.float32)
    return values.astype(ml_dtypes.bfloat16).astype(np.float32)


def squared_wave(length):
    indices = np.arange(length)
    folded = np.minimum(indices, length - indices)
    return (2.0 * math.pi / (length * spacing) * folded) ** 2


def coulomb_table():
    squares = (
        squared_wave(X)[:, None, None]
        + squared_wave(Y)[None, :, None]
        + squared_wave(Z)[None, None, :]
    )
    positive = squares > 0.0
    guarded = np.where(positive, squares, 1.0)
    screened = 4.0 * math.pi * (1.0 - np.exp(-guarded / (4.0 * screening * screening))) / guarded
    kernel = np.where(positive, screened, math.pi / (screening * screening))
    spread = np.sqrt(np.mean(kernel * kernel))
    return kernel / (spread * (X * Y * Z))


def tables(copies):
    table_z = np.einsum("zw,ab,pq->pazbqw", hartley(Z), np.eye(FOLD), np.eye(copies))
    table_z = table_z.reshape(copies * LANES, FOLD * copies * Z)
    table_x = np.kron(hartley(X), np.eye(EIGHT))
    h_y = hartley(Y).reshape(GROUPS_Y, EIGHT, FOLD, GROUPS_Y, EIGHT, FOLD)
    table_y = np.einsum("gjahkb,xw->agxjbhwk", h_y, np.eye(X_BLOCK))
    table_y = table_y.reshape(GROUPS * BLOCK_ROWS, GROUPS * BLOCK_ROWS)
    kernel = coulomb_table().reshape(X_BLOCKS, X_BLOCK, GROUPS_Y, EIGHT, FOLD, Z)
    kernel = np.transpose(kernel, (0, 4, 2, 1, 3, 5)).reshape(X_BLOCKS, GROUPS * BLOCK_ROWS, Z)
    kernel = np.tile(kernel, (1, 1, copies))
    narrow = ml_dtypes.bfloat16
    return (
        table_z.astype(narrow),
        np.ascontiguousarray(table_z.T).astype(narrow),
        table_x.astype(narrow),
        table_y.astype(narrow),
        kernel.astype(np.float32),
    )


def body(
    n_orb, n_grp, factor,
    target, own, table_z, table_zt, table_x, table_y, kernel,
    out,
    slots, wide, narrow, total, outbox, inbox,
    send_sems, recv_sems, forward_sems, out_sems, in_sems,
):
    me = lax.axis_index("orb")
    group = lax.axis_index("grp")
    copies = own.shape[0]
    slab = X // n_grp
    slab_rows = slab * ROWS_Y
    padded = outbox.shape[1]

    barrier = pltpu.get_barrier_semaphore()
    orb_steps = sorted({d % n_orb for d in (1, 2, -1, -2)} - {0})
    for distance in orb_steps:
        pl.semaphore_signal(
            barrier, inc=1, device_id=(lax.rem(me + distance, n_orb), group),
            device_id_type=pl.DeviceIdType.MESH,
        )
    for distance in range(1, n_grp):
        pl.semaphore_signal(
            barrier, inc=1, device_id=(me, lax.rem(group + distance, n_grp)),
            device_id_type=pl.DeviceIdType.MESH,
        )
    pl.semaphore_wait(barrier, len(orb_steps) + n_grp - 1)

    def remote(source, slot, p, distance, sems):
        return pltpu.make_async_remote_copy(
            src_ref=source.at[p],
            dst_ref=slots.at[slot, p],
            send_sem=sems.at[p],
            recv_sem=recv_sems.at[slot, p],
            device_id=(lax.rem(me + distance, n_orb), group),
            device_id_type=pl.DeviceIdType.MESH,
        )

    first = [remote(own, 0, p, 1, send_sems.at[0]) for p in range(copies)]
    forward = [remote(slots.at[0], 1, p, 1, forward_sems) for p in range(copies)]
    direct = [remote(own, 1, p, 2, send_sems.at[1]) for p in range(copies)]
    for copy in first:
        copy.start()

    def dot(a, b):
        return jnp.dot(a, b, preferred_element_type=f32)

    def to_spectrum_and_back(partners):
        for at in range(X_BLOCKS):
            rows = slice(at * X_BLOCK * ROWS_Y, (at + 1) * X_BLOCK * ROWS_Y)
            trial = target[rows].astype(f32)
            density = jnp.concatenate(
                [(trial * partners[p, rows].astype(f32)).astype(bf16) for p in range(copies)],
                axis=1,
            )
            wide[at * X_BLOCK : (at + 1) * X_BLOCK] = dot(density, table_z[...]).reshape(
                X_BLOCK, ROWS_Y, FOLD * LANES
            )
        for g in range(GROUPS):
            half, low = g // GROUPS_Y, g % GROUPS_Y * EIGHT
            field = wide[:, low : low + EIGHT, half * LANES : (half + 1) * LANES]
            field = dot(table_x[...], field.reshape(X * EIGHT, LANES).astype(bf16)).astype(bf16)
            narrow[:, g] = field.reshape(X_BLOCKS, BLOCK_ROWS, LANES)
        for at in range(X_BLOCKS):
            field = narrow[at].reshape(GROUPS * BLOCK_ROWS, LANES)
            scaled = (dot(table_y[...], field) * kernel[at]).astype(bf16)
            scaled = dot(table_y[...], scaled).astype(bf16)
            narrow[at] = scaled.reshape(GROUPS, BLOCK_ROWS, LANES)
        for g in range(GROUPS):
            half, low = g // GROUPS_Y, g % GROUPS_Y * EIGHT
            field = dot(table_x[...], narrow[:, g].reshape(X * EIGHT, LANES))
            wide[:, low : low + EIGHT, half * LANES : (half + 1) * LANES] = field.reshape(
                X, EIGHT, LANES
            )

    def terms(partners, first_plane, planes):
        rows = pl.ds(first_plane * ROWS_Y, planes * ROWS_Y)
        field = wide[pl.ds(first_plane, planes)].reshape(planes * ROWS_Y, FOLD * LANES)
        field = dot(field.astype(bf16), table_zt[...])
        result = None
        for p in range(copies):
            term = field[:, p * LANES : (p + 1) * LANES] * partners[p, rows].astype(f32)
            result = term if result is None else result + term
        return result

    to_spectrum_and_back(own)
    for at in range(X_BLOCKS):
        rows = slice(at * X_BLOCK * ROWS_Y, (at + 1) * X_BLOCK * ROWS_Y)
        total[rows] = terms(own, at * X_BLOCK, X_BLOCK)

    for copy in first:
        copy.wait_recv()

    even = lax.rem(me, 2) == 0

    @pl.when(even)
    def _():
        for copy in direct:
            copy.start()
        for copy in forward:
            copy.start()

    to_spectrum_and_back(slots.at[0])
    for at in range(X_BLOCKS):
        rows = slice(at * X_BLOCK * ROWS_Y, (at + 1) * X_BLOCK * ROWS_Y)
        total[rows] += terms(slots.at[0], at * X_BLOCK, X_BLOCK)

    for copy in direct:
        copy.wait_recv()

    to_spectrum_and_back(slots.at[1])

    def summed(owner):
        rows = pl.ds(owner * slab_rows, slab_rows)
        return total[rows] + terms(slots.at[1], owner * slab, slab)

    sent = []
    for distance in range(1, n_grp):
        owner = lax.rem(group + distance, n_grp)
        outbox[distance - 1, 0:slab_rows] = (summed(owner) * factor).astype(bf16)
        if padded > slab_rows:
            outbox[distance - 1, slab_rows:padded] = jnp.zeros((padded - slab_rows, LANES), bf16)
        copy = pltpu.make_async_remote_copy(
            src_ref=outbox.at[distance - 1],
            dst_ref=inbox.at[distance - 1],
            send_sem=out_sems.at[distance - 1],
            recv_sem=in_sems.at[distance - 1],
            device_id=(me, owner),
            device_id_type=pl.DeviceIdType.MESH,
        )
        copy.start()
        sent.append(copy)
    result = summed(group) * factor
    for distance in range(1, n_grp):
        sent[distance - 1].wait_recv()
        result = result + inbox[distance - 1, 0:slab_rows].astype(f32)
    out[...] = result

    for copy in first + sent:
        copy.wait_send()

    @pl.when(even)
    def _():
        for copy in direct + forward:
            copy.wait_send()


def local(n_orb, n_grp, targets, partners):
    copies = partners.shape[0]
    rows = X * ROWS_Y
    slab_rows = rows // n_grp
    padded = -(-slab_rows // 16) * 16
    factor = -1.0 / math.sqrt(STEPS * n_grp * copies)
    constants = tables(copies)
    vmem = pl.BlockSpec(memory_space=pltpu.VMEM)
    result = pl.pallas_call(
        functools.partial(body, n_orb, n_grp, factor),
        out_shape=jax.ShapeDtypeStruct((slab_rows, LANES), f32),
        in_specs=[vmem] * 7,
        out_specs=vmem,
        scratch_shapes=[
            pltpu.VMEM((2, copies, rows, LANES), bf16),
            pltpu.VMEM((X, ROWS_Y, FOLD * LANES), f32),
            pltpu.VMEM((X_BLOCKS, GROUPS, BLOCK_ROWS, LANES), bf16),
            pltpu.VMEM((rows, LANES), f32),
            pltpu.VMEM((n_grp - 1, padded, LANES), bf16),
            pltpu.VMEM((n_grp - 1, padded, LANES), bf16),
            pltpu.SemaphoreType.DMA((2, copies)),
            pltpu.SemaphoreType.DMA((2, copies)),
            pltpu.SemaphoreType.DMA((copies,)),
            pltpu.SemaphoreType.DMA((n_grp - 1,)),
            pltpu.SemaphoreType.DMA((n_grp - 1,)),
        ],
        compiler_params=pltpu.CompilerParams(
            collective_id=0, has_side_effects=True, vmem_limit_bytes=32 * 1024 * 1024
        ),
    )(
        targets.reshape(rows, LANES),
        partners.reshape(copies, rows, LANES),
        *[jnp.asarray(table) for table in constants],
    )
    return result.reshape(1, slab_rows * LANES)


def solution(mesh):
    in_specs = (P("orb", None), P(("orb", "grp"), None))
    out_specs = P("orb", "grp")
    return jax.shard_map(
        functools.partial(local, mesh.shape["orb"], mesh.shape["grp"]),
        mesh=mesh, in_specs=in_specs, out_specs=out_specs, check_vma=False,
    )
```

time: 158 us -> 28.6 us (0.18)
  waiting for transfers between devices: 77.1 us -> 0 us
  local copies, waits for them, and re-layouts: 27.2 us -> 1.75 us
  Pallas kernels: 0 us -> 24.5 us
  other arithmetic: 26.3 us -> 2.15 us
  between operations: 15 us -> 0.07 us
  matrix products: 10.6 us -> 0 us
    unnamed x2 -> x0, waiting for transfers between devices: 72.3 us -> none
    pallas_call x0 -> x1, Pallas kernels: none -> 24.5 us  [local(): pl.pallas_call(functools.partial(body, n_orb, n_grp, factor), out_shape=j...]
    reduce_sum x4 -> x0, other arithmetic: 15 us -> none  [the longest x3 14 us: exchange_terms(): return jnp.sum(potential * partner_grid[:, :, None], axis=3)]
    convert_element_type x8 -> x0, local copies, waits for them, and re-layouts: 14.7 us -> none  [the longest x3 8.89 us: exchange_terms(): potential = scaled.reshape(X, Y, trials, copies, Z).astype(jnp.float32)]
    dot_general x18 -> x0, matrix products: 10.6 us -> none  [the longest x12 7.01 us: contract(): lax.dot_general(table, field, (((1,), (axis_number,)), ((), ())), preferr...]
    convert_element_type x2 -> x0, other arithmetic: 9.59 us -> none  [the longest x1 8.48 us: exchange_terms(): (target_grid * partner_grid[None]).astype(jnp.bfloat16)]
    another operation x5 -> x0, local copies, waits for them, and re-layouts: 9.25 us -> none
    ppermute x2 -> x0, waiting for transfers between devices: 4.87 us -> none  [from_behind(): return lax.ppermute(block, axis, route)]
  transfers between devices with their start and end apart: 3 -> 0, of which waited for: 3 -> 0; matrix products, arithmetic and copies ran while one was open for 6% -> 0% of each run, Pallas kernels for 0% -> 0%
where the time goes in v1:
time: 28.6 us; the launch traced here: 28.5 us
  Pallas kernels  24.5 us (86%)
  other arithmetic  2.15 us (8%)
  local copies, waits for them, and re-layouts  1.75 us (6%)
    pallas_call x1, Pallas kernels, local(): pl.pallas_call(functools.partial(body, n_orb, n_grp, factor), out_shape=j...  24.5 us
    unnamed x1, other arithmetic  2.15 us
    unnamed x10, local copies, waits for them, and re-layouts  1.75 us

profile of v1, /device:TPU:0, one launch (start us, length us, event | category | flops | bytes accessed | tf_op | source)
XLA Modules:
  0.0 28.5 jit_solution(15393140999529680586)
XLA Ops:
  0.0 0.0 copy-start
  0.0 2.1 %reduce = bf16[98304]{0:T(1024)(128)(2,1)S(1)} reduce(bf16[1,98304]{1,0:T(2,128)(2,1)} %param.7, bf16[]{:T(256)} %constant.14), dimensions={0}, to_apply=%param.7.reduce_sub_computation | reduce | bytes 393218 | tf_op args[0]
  2.2 0.0 copy-start.1
  2.2 0.0 copy-start.2
  2.2 0.0 copy-start.3
  2.2 1.1 %copy.10 = bf16[1,2,768,128]{3,2,1,0:T(8,128)(2,1)S(1)} copy(bf16[1,2,768,128]{3,1,2,0:T(2,128)(2,1)} %bitcast.9) | data formatting | bytes 786432
  3.3 0.0 copy-done
  3.3 0.0 copy-done.1
  3.3 0.0 copy-done.2
  3.3 0.0 copy-done.3
  3.3 24.5 %shard_map.73 = f32[96,128]{1,0:T(8,128)S(1)} custom-call(bf16[768,128]{1,0:T(8,128)(2,1)S(1)} %bitcast.7, bf16[2,768,128]{2,1,0:T(8,128)(2,1)S(1)} %bitcast.6, bf16[256,256]{1,0:T(8,128)(2,1)S(1)} %copy-done.1, bf16[256,256]{1,0:T(8,128)(2,1)S(1)} %copy-done.1, bf16[256,256]{1,0:T(8,128)(2,1)S(1)} %copy-done.2, bf16[192,192]{1,0:T(8,128)(2,1)S(1)} %copy-done.3, ...), custom_call_target="tpu_custom_call" | custom-call | tf_op jit(solution)/shard_map/pallas_call | solution.py:235
  27.8 0.6 %copy.12 = f32[1,12288]{1,0:T(1,128)} copy(f32[1,12288]{1,0:T(1,128)S(1)} %bitcast.8) | data formatting | bytes 98304
Async XLA Ops:
  0.0 3.3 %copy-start = (f32[8,192,128]{2,1,0:T(8,128)S(1)}, f32[8,192,128]{2,1,0:T(8,128)}, u32[]{:S(2)}) copy-start(f32[8,192,128]{2,1,0:T(8,128)} %constant.11.clone.kernel) | copy-start | bytes 2359300
  2.2 1.2 %copy-start.1 = (bf16[256,256]{1,0:T(8,128)(2,1)S(1)}, bf16[256,256]{1,0:T(8,128)(2,1)}, u32[]{:S(2)}) copy-start(bf16[256,256]{1,0:T(8,128)(2,1)} %constant.8.clone.table_z.table_zt) | copy-start | bytes 393220
  2.2 1.2 %copy-start.2 = (bf16[256,256]{1,0:T(8,128)(2,1)S(1)}, bf16[256,256]{1,0:T(8,128)(2,1)}, u32[]{:S(2)}) copy-start(bf16[256,256]{1,0:T(8,128)(2,1)} %constant.9.clone.table_x) | copy-start | bytes 393220
  2.2 1.1 %copy-start.3 = (bf16[192,192]{1,0:T(8,128)(2,1)S(1)}, bf16[192,192]{1,0:T(8,128)(2,1)}, u32[]{:S(2)}) copy-start(bf16[192,192]{1,0:T(8,128)(2,1)} %constant.10.clone.table_y) | copy-start | bytes 221188

commit v2 on v1

--- a/solution.py
+++ b/solution.py
@@ -81,8 +81,9 @@
     n_orb, n_grp, factor,
     target, own, table_z, table_zt, table_x, table_y, kernel,
     out,
-    slots, wide, narrow, total, outbox, inbox,
-    send_sems, recv_sems, forward_sems, out_sems, in_sems,
+    trials, pool, wide, narrow, total, kept, outbox, inbox, early_outbox, early_inbox, crossing,
+    local_sems, first_sems, slot_sems, forward_sems, trial_sems,
+    out_sems, in_sems, early_out_sems, early_in_sems, cross_sems,
 ):
     me = lax.axis_index("orb")
     group = lax.axis_index("grp")
@@ -90,13 +91,22 @@
     slab = X // n_grp
     slab_rows = slab * ROWS_Y
     padded = outbox.shape[1]
+    odd_index = lax.rem(me, 2)
+    even = odd_index == 0
+
+    def block_ahead(distance):
+        return (lax.rem(me + distance, n_orb), group)
+
+    own_copy = pltpu.make_async_copy(own, pool.at[0], local_sems.at[0])
+    target_copy = pltpu.make_async_copy(target.at[0], trials.at[0], local_sems.at[1])
+    own_copy.start()
+    target_copy.start()
 
     barrier = pltpu.get_barrier_semaphore()
     orb_steps = sorted({d % n_orb for d in (1, 2, -1, -2)} - {0})
     for distance in orb_steps:
         pl.semaphore_signal(
-            barrier, inc=1, device_id=(lax.rem(me + distance, n_orb), group),
-            device_id_type=pl.DeviceIdType.MESH,
+            barrier, inc=1, device_id=block_ahead(distance), device_id_type=pl.DeviceIdType.MESH
         )
     for distance in range(1, n_grp):
         pl.semaphore_signal(
@@ -105,29 +115,43 @@
         )
     pl.semaphore_wait(barrier, len(orb_steps) + n_grp - 1)
 
-    def remote(source, slot, p, distance, sems):
+    def remote(source, destination, send_sem, recv_sem, device):
         return pltpu.make_async_remote_copy(
-            src_ref=source.at[p],
-            dst_ref=slots.at[slot, p],
-            send_sem=sems.at[p],
-            recv_sem=recv_sems.at[slot, p],
-            device_id=(lax.rem(me + distance, n_orb), group),
-            device_id_type=pl.DeviceIdType.MESH,
-        )
-
-    first = [remote(own, 0, p, 1, send_sems.at[0]) for p in range(copies)]
-    forward = [remote(slots.at[0], 1, p, 1, forward_sems) for p in range(copies)]
-    direct = [remote(own, 1, p, 2, send_sems.at[1]) for p in range(copies)]
+            src_ref=source, dst_ref=destination, send_sem=send_sem, recv_sem=recv_sem,
+            device_id=device, device_id_type=pl.DeviceIdType.MESH,
+        )
+
+    trial_copy = remote(
+        target.at[0], trials.at[1], trial_sems.at[0], trial_sems.at[1], block_ahead(2)
+    )
+    first = [
+        remote(own.at[p], pool.at[1, p], first_sems.at[p], slot_sems.at[0, p], block_ahead(1))
+        for p in range(copies)
+    ]
+    forward = [
+        remote(
+            pool.at[1, p], pool.at[2, p], forward_sems.at[p], slot_sems.at[1, p], block_ahead(1)
+        )
+        for p in range(copies)
+    ]
+    cross_copy = remote(
+        crossing.at[0], crossing.at[1], cross_sems.at[0], cross_sems.at[1], block_ahead(2)
+    )
+
+    @pl.when(even)
+    def _():
+        trial_copy.start()
+
     for copy in first:
         copy.start()
 
     def dot(a, b):
         return jnp.dot(a, b, preferred_element_type=f32)
 
-    def to_spectrum_and_back(partners):
+    def to_spectrum_and_back(trial_rows, partners):
         for at in range(X_BLOCKS):
             rows = slice(at * X_BLOCK * ROWS_Y, (at + 1) * X_BLOCK * ROWS_Y)
-            trial = target[rows].astype(f32)
+            trial = trial_rows[rows].astype(f32)
             density = jnp.concatenate(
                 [(trial * partners[p, rows].astype(f32)).astype(bf16) for p in range(copies)],
                 axis=1,
@@ -162,65 +186,101 @@
             result = term if result is None else result + term
         return result
 
-    to_spectrum_and_back(own)
+    def put(place, value):
+        place[0:slab_rows] = value.astype(bf16)
+        if padded > slab_rows:
+            place[slab_rows:padded] = jnp.zeros((padded - slab_rows, LANES), bf16)
+
+    def to_owner(source, destination, sends, arrivals, distance):
+        return remote(
+            source.at[distance - 1], destination.at[distance - 1],
+            sends.at[distance - 1], arrivals.at[distance - 1],
+            (me, lax.rem(group + distance, n_grp)),
+        )
+
+    early = [
+        to_owner(early_outbox, early_inbox, early_out_sems, early_in_sems, distance)
+        for distance in range(1, n_grp)
+    ]
+    late = [
+        to_owner(outbox, inbox, out_sems, in_sems, distance) for distance in range(1, n_grp)
+    ]
+
+    to_spectrum_and_back(target.at[0], own)
     for at in range(X_BLOCKS):
         rows = slice(at * X_BLOCK * ROWS_Y, (at + 1) * X_BLOCK * ROWS_Y)
         total[rows] = terms(own, at * X_BLOCK, X_BLOCK)
 
-    for copy in first:
-        copy.wait_recv()
-
-    even = lax.rem(me, 2) == 0
-
-    @pl.when(even)
-    def _():
-        for copy in direct:
-            copy.start()
+    own_copy.wait()
+    target_copy.wait()
+
+    @pl.when(even)
+    def _():
+        trial_copy.wait_recv()
+
+    @pl.when(jnp.logical_not(even))
+    def _():
+        for copy in first:
+            copy.wait_recv()
+
+    middle = pool.at[odd_index]
+    to_spectrum_and_back(trials.at[1 - odd_index], middle)
+
+    @pl.when(even)
+    def _():
+        for distance in range(1, n_grp):
+            owner = lax.rem(group + distance, n_grp)
+            put(early_outbox.at[distance - 1], terms(middle, owner * slab, slab) * factor)
+            early[distance - 1].start()
+        kept[...] = terms(middle, group * slab, slab) * factor
+        for copy in first:
+            copy.wait_recv()
         for copy in forward:
             copy.start()
 
-    to_spectrum_and_back(slots.at[0])
-    for at in range(X_BLOCKS):
-        rows = slice(at * X_BLOCK * ROWS_Y, (at + 1) * X_BLOCK * ROWS_Y)
-        total[rows] += terms(slots.at[0], at * X_BLOCK, X_BLOCK)
-
-    for copy in direct:
-        copy.wait_recv()
-
-    to_spectrum_and_back(slots.at[1])
+    @pl.when(jnp.logical_not(even))
+    def _():
+        for at in range(X_BLOCKS):
+            rows = slice(at * X_BLOCK * ROWS_Y, (at + 1) * X_BLOCK * ROWS_Y)
+            total[rows] += terms(middle, at * X_BLOCK, X_BLOCK)
+        for copy in forward:
+            copy.wait_recv()
+
+    last = pool.at[1 + odd_index]
+    to_spectrum_and_back(target.at[0], last)
 
     def summed(owner):
         rows = pl.ds(owner * slab_rows, slab_rows)
-        return total[rows] + terms(slots.at[1], owner * slab, slab)
-
-    sent = []
+        return (total[rows] + terms(last, owner * slab, slab)) * factor
+
     for distance in range(1, n_grp):
-        owner = lax.rem(group + distance, n_grp)
-        outbox[distance - 1, 0:slab_rows] = (summed(owner) * factor).astype(bf16)
-        if padded > slab_rows:
-            outbox[distance - 1, slab_rows:padded] = jnp.zeros((padded - slab_rows, LANES), bf16)
-        copy = pltpu.make_async_remote_copy(
-            src_ref=outbox.at[distance - 1],
-            dst_ref=inbox.at[distance - 1],
-            send_sem=out_sems.at[distance - 1],
-            recv_sem=in_sems.at[distance - 1],
-            device_id=(me, owner),
-            device_id_type=pl.DeviceIdType.MESH,
-        )
-        copy.start()
-        sent.append(copy)
-    result = summed(group) * factor
+        put(outbox.at[distance - 1], summed(lax.rem(group + distance, n_grp)))
+        late[distance - 1].start()
+    out[...] = summed(group)
+
+    @pl.when(even)
+    def _():
+        crossed = kept[...]
+        for distance in range(1, n_grp):
+            early[distance - 1].wait_recv()
+            crossed = crossed + early_inbox[distance - 1, 0:slab_rows].astype(f32)
+        put(crossing.at[0], crossed)
+        cross_copy.start()
+
+    result = out[...]
     for distance in range(1, n_grp):
-        sent[distance - 1].wait_recv()
+        late[distance - 1].wait_recv()
         result = result + inbox[distance - 1, 0:slab_rows].astype(f32)
     out[...] = result
 
-    for copy in first + sent:
+    for copy in first + late:
         copy.wait_send()
 
     @pl.when(even)
     def _():
-        for copy in direct + forward:
+        cross_copy.wait_recv()
+        out[...] += crossing[1, 0:slab_rows].astype(f32)
+        for copy in forward + early + [trial_copy, cross_copy]:
             copy.wait_send()
 
 
@@ -232,29 +292,30 @@
     factor = -1.0 / math.sqrt(STEPS * n_grp * copies)
     constants = tables(copies)
     vmem = pl.BlockSpec(memory_space=pltpu.VMEM)
+    box = pltpu.VMEM((n_grp - 1, padded, LANES), bf16)
+    dma = pltpu.SemaphoreType.DMA
     result = pl.pallas_call(
         functools.partial(body, n_orb, n_grp, factor),
         out_shape=jax.ShapeDtypeStruct((slab_rows, LANES), f32),
         in_specs=[vmem] * 7,
         out_specs=vmem,
         scratch_shapes=[
-            pltpu.VMEM((2, copies, rows, LANES), bf16),
+            pltpu.VMEM((2, rows, LANES), bf16),
+            pltpu.VMEM((3, copies, rows, LANES), bf16),
             pltpu.VMEM((X, ROWS_Y, FOLD * LANES), f32),
             pltpu.VMEM((X_BLOCKS, GROUPS, BLOCK_ROWS, LANES), bf16),
             pltpu.VMEM((rows, LANES), f32),
-            pltpu.VMEM((n_grp - 1, padded, LANES), bf16),
-            pltpu.VMEM((n_grp - 1, padded, LANES), bf16),
-            pltpu.SemaphoreType.DMA((2, copies)),
-            pltpu.SemaphoreType.DMA((2, copies)),
-            pltpu.SemaphoreType.DMA((copies,)),
-            pltpu.SemaphoreType.DMA((n_grp - 1,)),
-            pltpu.SemaphoreType.DMA((n_grp - 1,)),
+            pltpu.VMEM((slab_rows, LANES), f32),
+            box, box, box, box,
+            pltpu.VMEM((2, padded, LANES), bf16),
+            dma((2,)), dma((copies,)), dma((2, copies)), dma((copies,)), dma((2,)),
+            dma((n_grp - 1,)), dma((n_grp - 1,)), dma((n_grp - 1,)), dma((n_grp - 1,)), dma((2,)),
         ],
         compiler_params=pltpu.CompilerParams(
             collective_id=0, has_side_effects=True, vmem_limit_bytes=32 * 1024 * 1024
         ),
     )(
-        targets.reshape(rows, LANES),
+        targets.reshape(1, rows, LANES),
         partners.reshape(copies, rows, LANES),
         *[jnp.asarray(table) for table in constants],
     )

time: 28.6 us -> 27.6 us (0.965)
  Pallas kernels: 24.5 us -> 23.2 us
    pallas_call x1, Pallas kernels: 24.5 us -> 23.2 us  [local(): pl.pallas_call(functools.partial(body, n_orb, n_grp, factor), out_shape=j...]
where the time goes in v2:
time: 27.6 us; the launch traced here: 27.2 us
  Pallas kernels  23.2 us (84%)
  other arithmetic  2.15 us (8%)
  local copies, waits for them, and re-layouts  1.75 us (6%)
    pallas_call x1, Pallas kernels, local(): pl.pallas_call(functools.partial(body, n_orb, n_grp, factor), out_shape=j...  23.2 us
    unnamed x1, other arithmetic  2.15 us
    unnamed x10, local copies, waits for them, and re-layouts  1.75 us

profile of v2, /device:TPU:0, one launch (start us, length us, event | category | flops | bytes accessed | tf_op | source)
XLA Modules:
  0.0 27.2 jit_solution(11349934573343794144)
XLA Ops:
  0.0 0.0 copy-start
  0.0 2.1 %reduce = bf16[98304]{0:T(1024)(128)(2,1)S(1)} reduce(bf16[1,98304]{1,0:T(2,128)(2,1)} %param.7, bf16[]{:T(256)} %constant.14), dimensions={0}, to_apply=%param.7.reduce_sub_computation | reduce | bytes 393218 | tf_op args[0]
  2.2 0.0 copy-start.1
  2.2 0.0 copy-start.2
  2.2 0.0 copy-start.3
  2.2 1.1 %copy.10 = bf16[1,2,768,128]{3,2,1,0:T(8,128)(2,1)S(1)} copy(bf16[1,2,768,128]{3,1,2,0:T(2,128)(2,1)} %bitcast.9) | data formatting | bytes 786432
  3.3 0.0 copy-done
  3.3 0.0 copy-done.1
  3.3 0.0 copy-done.2
  3.3 0.0 copy-done.3
  3.3 23.2 %shard_map.73 = f32[96,128]{1,0:T(8,128)S(1)} custom-call(bf16[1,768,128]{2,1,0:T(8,128)(2,1)S(1)} %bitcast.7, bf16[2,768,128]{2,1,0:T(8,128)(2,1)S(1)} %bitcast.6, bf16[256,256]{1,0:T(8,128)(2,1)S(1)} %copy-done.1, bf16[256,256]{1,0:T(8,128)(2,1)S(1)} %copy-done.1, bf16[256,256]{1,0:T(8,128)(2,1)S(1)} %copy-done.2, bf16[192,192]{1,0:T(8,128)(2,1)S(1)} %copy-done.3, ...), custom_call_target="tpu_custom_call" | custom-call | tf_op jit(solution)/shard_map/pallas_call | solution.py:297
  26.6 0.6 %copy.12 = f32[1,12288]{1,0:T(1,128)} copy(f32[1,12288]{1,0:T(1,128)S(1)} %bitcast.8) | data formatting | bytes 98304
Async XLA Ops:
  0.0 3.3 %copy-start = (f32[8,192,128]{2,1,0:T(8,128)S(1)}, f32[8,192,128]{2,1,0:T(8,128)}, u32[]{:S(2)}) copy-start(f32[8,192,128]{2,1,0:T(8,128)} %constant.11.clone.kernel) | copy-start | bytes 2359300
  2.2 1.2 %copy-start.1 = (bf16[256,256]{1,0:T(8,128)(2,1)S(1)}, bf16[256,256]{1,0:T(8,128)(2,1)}, u32[]{:S(2)}) copy-start(bf16[256,256]{1,0:T(8,128)(2,1)} %constant.8.clone.table_z.table_zt) | copy-start | bytes 393220
  2.2 1.2 %copy-start.2 = (bf16[256,256]{1,0:T(8,128)(2,1)S(1)}, bf16[256,256]{1,0:T(8,128)(2,1)}, u32[]{:S(2)}) copy-start(bf16[256,256]{1,0:T(8,128)(2,1)} %constant.9.clone.table_x) | copy-start | bytes 393220
  2.2 1.1 %copy-start.3 = (bf16[192,192]{1,0:T(8,128)(2,1)S(1)}, bf16[192,192]{1,0:T(8,128)(2,1)}, u32[]{:S(2)}) copy-start(bf16[192,192]{1,0:T(8,128)(2,1)} %constant.10.clone.table_y) | copy-start | bytes 221188

commit v3 on v2

--- a/solution.py
+++ b/solution.py
@@ -81,9 +81,8 @@
     n_orb, n_grp, factor,
     target, own, table_z, table_zt, table_x, table_y, kernel,
     out,
-    trials, pool, wide, narrow, total, kept, outbox, inbox, early_outbox, early_inbox, crossing,
-    local_sems, first_sems, slot_sems, forward_sems, trial_sems,
-    out_sems, in_sems, early_out_sems, early_in_sems, cross_sems,
+    trials, pool, wide, narrow, total, outbox, inbox, far_outbox, far_inbox,
+    local_sem, swap_sems, trial_sems, out_sems, in_sems, far_out_sems, far_in_sems,
 ):
     me = lax.axis_index("orb")
     group = lax.axis_index("grp")
@@ -94,26 +93,24 @@
     odd_index = lax.rem(me, 2)
     even = odd_index == 0
 
-    def block_ahead(distance):
-        return (lax.rem(me + distance, n_orb), group)
-
-    own_copy = pltpu.make_async_copy(own, pool.at[0], local_sems.at[0])
-    target_copy = pltpu.make_async_copy(target.at[0], trials.at[0], local_sems.at[1])
+    sibling = (me + 1 - 2 * odd_index, group)
+    ahead = lax.rem(me + 2, n_orb)
+    behind = lax.rem(me + n_orb - 2, n_orb)
+
+    own_copy = pltpu.make_async_copy(own, pool.at[0], local_sem)
     own_copy.start()
-    target_copy.start()
 
     barrier = pltpu.get_barrier_semaphore()
-    orb_steps = sorted({d % n_orb for d in (1, 2, -1, -2)} - {0})
-    for distance in orb_steps:
+    met = [sibling]
+    for distance in range(n_grp):
+        other = lax.rem(group + distance, n_grp)
+        met += [(me, other)] * (distance > 0) + [(ahead, other)] + [(behind, other)] * (n_orb > 4)
+    for device in met:
         pl.semaphore_signal(
-            barrier, inc=1, device_id=block_ahead(distance), device_id_type=pl.DeviceIdType.MESH
+            barrier, inc=1, device_id=device, device_id_type=pl.DeviceIdType.MESH
         )
-    for distance in range(1, n_grp):
-        pl.semaphore_signal(
-            barrier, inc=1, device_id=(me, lax.rem(group + distance, n_grp)),
-            device_id_type=pl.DeviceIdType.MESH,
-        )
-    pl.semaphore_wait(barrier, len(orb_steps) + n_grp - 1)
+    trials[0] = target[...].astype(bf16)
+    pl.semaphore_wait(barrier, len(met))
 
     def remote(source, destination, send_sem, recv_sem, device):
         return pltpu.make_async_remote_copy(
@@ -122,27 +119,16 @@
         )
 
     trial_copy = remote(
-        target.at[0], trials.at[1], trial_sems.at[0], trial_sems.at[1], block_ahead(2)
-    )
-    first = [
-        remote(own.at[p], pool.at[1, p], first_sems.at[p], slot_sems.at[0, p], block_ahead(1))
+        trials.at[0], trials.at[1], trial_sems.at[0], trial_sems.at[1], (behind, group)
+    )
+    swap = [
+        remote(own.at[p], pool.at[1, p], swap_sems.at[0, p], swap_sems.at[1, p], sibling)
         for p in range(copies)
     ]
-    forward = [
-        remote(
-            pool.at[1, p], pool.at[2, p], forward_sems.at[p], slot_sems.at[1, p], block_ahead(1)
-        )
-        for p in range(copies)
-    ]
-    cross_copy = remote(
-        crossing.at[0], crossing.at[1], cross_sems.at[0], cross_sems.at[1], block_ahead(2)
-    )
-
-    @pl.when(even)
-    def _():
-        trial_copy.start()
-
-    for copy in first:
+
+    trial_copy.start()
+
+    for copy in swap:
         copy.start()
 
     def dot(a, b):
@@ -191,28 +177,52 @@
         if padded > slab_rows:
             place[slab_rows:padded] = jnp.zeros((padded - slab_rows, LANES), bf16)
 
-    def to_owner(source, destination, sends, arrivals, distance):
+    def to_owner(source, destination, sends, arrivals, orb, distance):
         return remote(
-            source.at[distance - 1], destination.at[distance - 1],
-            sends.at[distance - 1], arrivals.at[distance - 1],
-            (me, lax.rem(group + distance, n_grp)),
+            source.at[distance], destination.at[distance], sends.at[distance],
+            arrivals.at[distance], (orb, lax.rem(group + distance, n_grp)),
         )
 
-    early = [
-        to_owner(early_outbox, early_inbox, early_out_sems, early_in_sems, distance)
-        for distance in range(1, n_grp)
+    near = [
+        to_owner(outbox, inbox, out_sems, in_sems, me, distance) for distance in range(1, n_grp)
     ]
-    late = [
-        to_owner(outbox, inbox, out_sems, in_sems, distance) for distance in range(1, n_grp)
+    far = [
+        to_owner(far_outbox, far_inbox, far_out_sems, far_in_sems, ahead, distance)
+        for distance in range(n_grp)
     ]
 
-    to_spectrum_and_back(target.at[0], own)
-    for at in range(X_BLOCKS):
-        rows = slice(at * X_BLOCK * ROWS_Y, (at + 1) * X_BLOCK * ROWS_Y)
-        total[rows] = terms(own, at * X_BLOCK, X_BLOCK)
+    def store_total(partners):
+        for at in range(X_BLOCKS):
+            rows = slice(at * X_BLOCK * ROWS_Y, (at + 1) * X_BLOCK * ROWS_Y)
+            total[rows] = terms(partners, at * X_BLOCK, X_BLOCK)
+
+    def send_out(partners, add_total, box, sends, mine):
+        def summed(owner):
+            value = terms(partners, owner * slab, slab)
+            if add_total:
+                value = value + total[pl.ds(owner * slab_rows, slab_rows)]
+            return value * factor
+
+        for distance in range(1, n_grp):
+            put(box.at[distance], summed(lax.rem(group + distance, n_grp)))
+            sends[distance - n_grp].start()
+        if mine is None:
+            put(box.at[0], summed(group))
+            sends[0].start()
+        else:
+            mine[...] = summed(group)
+
+    to_spectrum_and_back(trials.at[0], own)
+
+    @pl.when(even)
+    def _():
+        send_out(own, False, outbox, near, out)
+
+    @pl.when(jnp.logical_not(even))
+    def _():
+        store_total(own)
 
     own_copy.wait()
-    target_copy.wait()
 
     @pl.when(even)
     def _():
@@ -220,7 +230,7 @@
 
     @pl.when(jnp.logical_not(even))
     def _():
-        for copy in first:
+        for copy in swap:
             copy.wait_recv()
 
     middle = pool.at[odd_index]
@@ -228,60 +238,30 @@
 
     @pl.when(even)
     def _():
-        for distance in range(1, n_grp):
-            owner = lax.rem(group + distance, n_grp)
-            put(early_outbox.at[distance - 1], terms(middle, owner * slab, slab) * factor)
-            early[distance - 1].start()
-        kept[...] = terms(middle, group * slab, slab) * factor
-        for copy in first:
+        store_total(middle)
+        for copy in swap:
             copy.wait_recv()
-        for copy in forward:
-            copy.start()
 
     @pl.when(jnp.logical_not(even))
     def _():
-        for at in range(X_BLOCKS):
-            rows = slice(at * X_BLOCK * ROWS_Y, (at + 1) * X_BLOCK * ROWS_Y)
-            total[rows] += terms(middle, at * X_BLOCK, X_BLOCK)
-        for copy in forward:
-            copy.wait_recv()
-
-    last = pool.at[1 + odd_index]
-    to_spectrum_and_back(target.at[0], last)
-
-    def summed(owner):
-        rows = pl.ds(owner * slab_rows, slab_rows)
-        return (total[rows] + terms(last, owner * slab, slab)) * factor
-
-    for distance in range(1, n_grp):
-        put(outbox.at[distance - 1], summed(lax.rem(group + distance, n_grp)))
-        late[distance - 1].start()
-    out[...] = summed(group)
-
-    @pl.when(even)
-    def _():
-        crossed = kept[...]
-        for distance in range(1, n_grp):
-            early[distance - 1].wait_recv()
-            crossed = crossed + early_inbox[distance - 1, 0:slab_rows].astype(f32)
-        put(crossing.at[0], crossed)
-        cross_copy.start()
+        send_out(middle, True, outbox, near, out)
+        total[...] = jnp.zeros_like(total)
+        trial_copy.wait_recv()
+
+    last = pool.at[1 - odd_index]
+    to_spectrum_and_back(trials.at[1], last)
+    send_out(last, True, far_outbox, far, None)
 
     result = out[...]
     for distance in range(1, n_grp):
-        late[distance - 1].wait_recv()
-        result = result + inbox[distance - 1, 0:slab_rows].astype(f32)
+        near[distance - 1].wait_recv()
+        result = result + inbox[distance, 0:slab_rows].astype(f32)
+    for distance in range(n_grp):
+        far[distance].wait_recv()
+        result = result + far_inbox[distance, 0:slab_rows].astype(f32)
     out[...] = result
-
-    for copy in first + late:
+    for copy in swap + near + far + [trial_copy]:
         copy.wait_send()
-
-    @pl.when(even)
-    def _():
-        cross_copy.wait_recv()
-        out[...] += crossing[1, 0:slab_rows].astype(f32)
-        for copy in forward + early + [trial_copy, cross_copy]:
-            copy.wait_send()
 
 
 def local(n_orb, n_grp, targets, partners):
@@ -292,7 +272,7 @@
     factor = -1.0 / math.sqrt(STEPS * n_grp * copies)
     constants = tables(copies)
     vmem = pl.BlockSpec(memory_space=pltpu.VMEM)
-    box = pltpu.VMEM((n_grp - 1, padded, LANES), bf16)
+    box = pltpu.VMEM((n_grp, padded, LANES), bf16)
     dma = pltpu.SemaphoreType.DMA
     result = pl.pallas_call(
         functools.partial(body, n_orb, n_grp, factor),
@@ -305,17 +285,15 @@
             pltpu.VMEM((X, ROWS_Y, FOLD * LANES), f32),
             pltpu.VMEM((X_BLOCKS, GROUPS, BLOCK_ROWS, LANES), bf16),
             pltpu.VMEM((rows, LANES), f32),
-            pltpu.VMEM((slab_rows, LANES), f32),
             box, box, box, box,
-            pltpu.VMEM((2, padded, LANES), bf16),
-            dma((2,)), dma((copies,)), dma((2, copies)), dma((copies,)), dma((2,)),
-            dma((n_grp - 1,)), dma((n_grp - 1,)), dma((n_grp - 1,)), dma((n_grp - 1,)), dma((2,)),
+            dma, dma((2, copies)), dma((2,)),
+            dma((n_grp,)), dma((n_grp,)), dma((n_grp,)), dma((n_grp,)),
         ],
         compiler_params=pltpu.CompilerParams(
             collective_id=0, has_side_effects=True, vmem_limit_bytes=32 * 1024 * 1024
         ),
     )(
-        targets.reshape(1, rows, LANES),
+        lax.optimization_barrier(targets.astype(f32)).reshape(rows, LANES),
         partners.reshape(copies, rows, LANES),
         *[jnp.asarray(table) for table in constants],
     )

time: 27.6 us -> 25.2 us (0.913)
  Pallas kernels: 23.2 us -> 21.8 us
  other arithmetic: 2.15 us -> 1.47 us
    unnamed x1 -> x0, other arithmetic: 2.15 us -> none
    pallas_call x1, Pallas kernels: 23.2 us -> 21.8 us  [local(): pl.pallas_call(functools.partial(body, n_orb, n_grp, factor), out_shape=j...]
    convert_element_type x0 -> x1, other arithmetic: none -> 1.47 us  [local(): targets.astype(f32)]
where the time goes in v3:
time: 25.2 us; the launch traced here: 25 us
  Pallas kernels  21.8 us (87%)
  local copies, waits for them, and re-layouts  1.75 us (7%)
  other arithmetic  1.47 us (6%)
    pallas_call x1, Pallas kernels, local(): pl.pallas_call(functools.partial(body, n_orb, n_grp, factor), out_shape=j...  21.8 us
    unnamed x10, local copies, waits for them, and re-layouts  1.75 us
    convert_element_type x1, other arithmetic, local(): targets.astype(f32)  1.47 us

profile of v3, /device:TPU:0, one launch (start us, length us, event | category | flops | bytes accessed | tf_op | source)
XLA Modules:
  0.0 25.0 jit_solution(15173383919503178466)
XLA Ops:
  0.0 0.0 copy-start
  0.0 1.5 %convert_element_type.3 = f32[1,98304]{1,0:T(1,128)S(1)} convert(bf16[1,98304]{1,0:T(2,128)(2,1)} %param.7) | non-fusion elementwise | flops 98304 | bytes 589824 | tf_op jit(solution)/shard_map/convert_element_type | solution.py:296
  1.5 0.0 copy-start.1
  1.5 0.0 copy-start.2
  1.5 0.0 copy-start.3
  1.5 1.1 %copy.10 = bf16[1,2,768,128]{3,2,1,0:T(8,128)(2,1)S(1)} copy(bf16[1,2,768,128]{3,1,2,0:T(2,128)(2,1)} %bitcast.9) | data formatting | bytes 786432
  2.6 0.0 copy-done
  2.6 0.0 copy-done.1
  2.6 0.0 copy-done.2
  2.7 0.0 copy-done.3
  2.7 21.8 %shard_map.73 = f32[96,128]{1,0:T(8,128)S(1)} custom-call(f32[768,128]{1,0:T(8,128)S(1)} %bitcast.6, bf16[2,768,128]{2,1,0:T(8,128)(2,1)S(1)} %bitcast.7, bf16[256,256]{1,0:T(8,128)(2,1)S(1)} %copy-done.1, bf16[256,256]{1,0:T(8,128)(2,1)S(1)} %copy-done.1, bf16[256,256]{1,0:T(8,128)(2,1)S(1)} %copy-done.2, bf16[192,192]{1,0:T(8,128)(2,1)S(1)} %copy-done.3, ...), custom_call_target="tpu_custom_call" | custom-call | tf_op jit(solution)/shard_map/pallas_call | solution.py:277
  24.4 0.6 %copy.12 = f32[1,12288]{1,0:T(1,128)} copy(f32[1,12288]{1,0:T(1,128)S(1)} %bitcast.8) | data formatting | bytes 98304
Async XLA Ops:
  0.0 2.6 %copy-start = (f32[8,192,128]{2,1,0:T(8,128)S(1)}, f32[8,192,128]{2,1,0:T(8,128)}, u32[]{:S(2)}) copy-start(f32[8,192,128]{2,1,0:T(8,128)} %constant.11.clone.kernel) | copy-start | bytes 2359300
  1.5 1.2 %copy-start.1 = (bf16[256,256]{1,0:T(8,128)(2,1)S(1)}, bf16[256,256]{1,0:T(8,128)(2,1)}, u32[]{:S(2)}) copy-start(bf16[256,256]{1,0:T(8,128)(2,1)} %constant.8.clone.table_z.table_zt) | copy-start | bytes 393220
  1.5 1.2 %copy-start.2 = (bf16[256,256]{1,0:T(8,128)(2,1)S(1)}, bf16[256,256]{1,0:T(8,128)(2,1)}, u32[]{:S(2)}) copy-start(bf16[256,256]{1,0:T(8,128)(2,1)} %constant.9.clone.table_x) | copy-start | bytes 393220
  1.5 1.1 %copy-start.3 = (bf16[192,192]{1,0:T(8,128)(2,1)S(1)}, bf16[192,192]{1,0:T(8,128)(2,1)}, u32[]{:S(2)}) copy-start(bf16[192,192]{1,0:T(8,128)(2,1)} %constant.10.clone.table_y) | copy-start | bytes 221188

commit v4 on v3

--- a/solution.py
+++ b/solution.py
@@ -137,29 +137,45 @@
     def to_spectrum_and_back(trial_rows, partners):
         for at in range(X_BLOCKS):
             rows = slice(at * X_BLOCK * ROWS_Y, (at + 1) * X_BLOCK * ROWS_Y)
-            trial = trial_rows[rows].astype(f32)
+            trial = trial_rows[rows]
             density = jnp.concatenate(
-                [(trial * partners[p, rows].astype(f32)).astype(bf16) for p in range(copies)],
+                [trial * partners[p, rows] for p in range(copies)],
                 axis=1,
             )
             wide[at * X_BLOCK : (at + 1) * X_BLOCK] = dot(density, table_z[...]).reshape(
                 X_BLOCK, ROWS_Y, FOLD * LANES
             )
-        for g in range(GROUPS):
-            half, low = g // GROUPS_Y, g % GROUPS_Y * EIGHT
-            field = wide[:, low : low + EIGHT, half * LANES : (half + 1) * LANES]
-            field = dot(table_x[...], field.reshape(X * EIGHT, LANES).astype(bf16)).astype(bf16)
-            narrow[:, g] = field.reshape(X_BLOCKS, BLOCK_ROWS, LANES)
-        for at in range(X_BLOCKS):
-            field = narrow[at].reshape(GROUPS * BLOCK_ROWS, LANES)
-            scaled = (dot(table_y[...], field) * kernel[at]).astype(bf16)
+        for g in range(GROUPS_Y):
+            low = g * EIGHT
+            field = wide[:, low : low + EIGHT].reshape(X * EIGHT, FOLD * LANES).astype(bf16)
+            field = dot(table_x[...], field).astype(bf16)
+            for half in range(FOLD):
+                narrow[:, half * GROUPS_Y + g] = field[
+                    :, half * LANES : (half + 1) * LANES
+                ].reshape(X_BLOCKS, BLOCK_ROWS, LANES)
+        for at in range(0, X_BLOCKS, 2):
+            two = (at, at + 1)
+            field = jnp.concatenate(
+                [narrow[b].reshape(GROUPS * BLOCK_ROWS, LANES) for b in two], axis=1
+            )
+            table = jnp.concatenate([kernel[b] for b in two], axis=1)
+            scaled = (dot(table_y[...], field) * table).astype(bf16)
             scaled = dot(table_y[...], scaled).astype(bf16)
-            narrow[at] = scaled.reshape(GROUPS, BLOCK_ROWS, LANES)
-        for g in range(GROUPS):
-            half, low = g // GROUPS_Y, g % GROUPS_Y * EIGHT
-            field = dot(table_x[...], narrow[:, g].reshape(X * EIGHT, LANES))
-            wide[:, low : low + EIGHT, half * LANES : (half + 1) * LANES] = field.reshape(
-                X, EIGHT, LANES
+            for i, b in enumerate(two):
+                narrow[b] = scaled[:, i * LANES : (i + 1) * LANES].reshape(
+                    GROUPS, BLOCK_ROWS, LANES
+                )
+        for g in range(GROUPS_Y):
+            low = g * EIGHT
+            field = jnp.concatenate(
+                [
+                    narrow[:, half * GROUPS_Y + g].reshape(X * EIGHT, LANES)
+                    for half in range(FOLD)
+                ],
+                axis=1,
+            )
+            wide[:, low : low + EIGHT] = dot(table_x[...], field).reshape(
+                X, EIGHT, FOLD * LANES
             )
 
     def terms(partners, first_plane, planes):

time: 25.2 us -> 24.6 us (0.976)
  Pallas kernels: 21.8 us -> 21.2 us
    pallas_call x1, Pallas kernels: 21.8 us -> 21.2 us  [local(): pl.pallas_call(functools.partial(body, n_orb, n_grp, factor), out_shape=j...]
where the time goes in v4:
time: 24.6 us; the launch traced here: 24.5 us
  Pallas kernels  21.2 us (86%)
  local copies, waits for them, and re-layouts  1.75 us (7%)
  other arithmetic  1.47 us (6%)
    pallas_call x1, Pallas kernels, local(): pl.pallas_call(functools.partial(body, n_orb, n_grp, factor), out_shape=j...  21.2 us
    unnamed x10, local copies, waits for them, and re-layouts  1.75 us
    convert_element_type x1, other arithmetic, local(): targets.astype(f32)  1.47 us

profile of v4, /device:TPU:0, one launch (start us, length us, event | category | flops | bytes accessed | tf_op | source)
XLA Modules:
  0.0 24.5 jit_solution(10709720405059165757)
XLA Ops:
  0.0 0.0 copy-start
  0.0 1.5 %convert_element_type.3 = f32[1,98304]{1,0:T(1,128)S(1)} convert(bf16[1,98304]{1,0:T(2,128)(2,1)} %param.7) | non-fusion elementwise | flops 98304 | bytes 589824 | tf_op jit(solution)/shard_map/convert_element_type | solution.py:312
  1.5 0.0 copy-start.1
  1.5 0.0 copy-start.2
  1.5 0.0 copy-start.3
  1.5 1.1 %copy.10 = bf16[1,2,768,128]{3,2,1,0:T(8,128)(2,1)S(1)} copy(bf16[1,2,768,128]{3,1,2,0:T(2,128)(2,1)} %bitcast.9) | data formatting | bytes 786432
  2.6 0.0 copy-done
  2.6 0.0 copy-done.1
  2.6 0.0 copy-done.2
  2.7 0.0 copy-done.3
  2.7 21.2 %shard_map.73 = f32[96,128]{1,0:T(8,128)S(1)} custom-call(f32[768,128]{1,0:T(8,128)S(1)} %bitcast.6, bf16[2,768,128]{2,1,0:T(8,128)(2,1)S(1)} %bitcast.7, bf16[256,256]{1,0:T(8,128)(2,1)S(1)} %copy-done.1, bf16[256,256]{1,0:T(8,128)(2,1)S(1)} %copy-done.1, bf16[256,256]{1,0:T(8,128)(2,1)S(1)} %copy-done.2, bf16[192,192]{1,0:T(8,128)(2,1)S(1)} %copy-done.3, ...), custom_call_target="tpu_custom_call" | custom-call | tf_op jit(solution)/shard_map/pallas_call | solution.py:293
  23.9 0.6 %copy.12 = f32[1,12288]{1,0:T(1,128)} copy(f32[1,12288]{1,0:T(1,128)S(1)} %bitcast.8) | data formatting | bytes 98304
Async XLA Ops:
  0.0 2.6 %copy-start = (f32[8,192,128]{2,1,0:T(8,128)S(1)}, f32[8,192,128]{2,1,0:T(8,128)}, u32[]{:S(2)}) copy-start(f32[8,192,128]{2,1,0:T(8,128)} %constant.11.clone.kernel) | copy-start | bytes 2359300
  1.5 1.2 %copy-start.1 = (bf16[256,256]{1,0:T(8,128)(2,1)S(1)}, bf16[256,256]{1,0:T(8,128)(2,1)}, u32[]{:S(2)}) copy-start(bf16[256,256]{1,0:T(8,128)(2,1)} %constant.8.clone.table_z.table_zt) | copy-start | bytes 393220
  1.5 1.2 %copy-start.2 = (bf16[256,256]{1,0:T(8,128)(2,1)S(1)}, bf16[256,256]{1,0:T(8,128)(2,1)}, u32[]{:S(2)}) copy-start(bf16[256,256]{1,0:T(8,128)(2,1)} %constant.9.clone.table_x) | copy-start | bytes 393220
  1.5 1.1 %copy-start.3 = (bf16[192,192]{1,0:T(8,128)(2,1)S(1)}, bf16[192,192]{1,0:T(8,128)(2,1)}, u32[]{:S(2)}) copy-start(bf16[192,192]{1,0:T(8,128)(2,1)} %constant.10.clone.table_y) | copy-start | bytes 221188
